TPU v7x, 32 devices: a whole 2x2x4 slice. The times are simulated.
32 devices in a mesh: pipe: 2 (over x), dp: 16 (over z, y, core).
Axes of the slice: x: 2, y: 2, z: 4, core: 2. Of those that a mesh axis runs over, the one named last changes fastest.
Arguments:
- frames: bfloat16 [2, 16, 384, 512], P(None, 'dp'), may hold values from -6 to 6
- cotangent: bfloat16 [2, 16, 384, 512], P(None, 'dp'), may hold values from -6 to 6
- lengths: int32 [2, 16], P(None, 'dp'), may hold values from 96 to 384, as said below
- stream_flags: int32 [2, 16], P(None, 'dp'), may hold values 0 or 1
- span_sizes: int32 [2, 16], P(None, 'dp'), may hold values from 24 to 96
- early_gain: bfloat16 [2, 512], P('pipe', 'dp'), may hold values from 0.25 to 1.75
- early_up: bfloat16 [2, 512, 2048], P('pipe', 'dp'), may hold values from -0.25 to 0.25
- early_down: bfloat16 [2, 2048, 512], P('pipe', None, 'dp'), may hold values from -0.125 to 0.125
- attend_gain: bfloat16 [2, 512], P('pipe', 'dp'), may hold values from 0.25 to 1.75
- attend_proj: bfloat16 [2, 512, 1536], P('pipe', 'dp'), may hold values from -0.25 to 0.25
- attend_out: bfloat16 [2, 512, 512], P('pipe', 'dp'), may hold values from -2 to 2
- convolve_gain: bfloat16 [2, 512], P('pipe', 'dp'), may hold values from 0.25 to 1.75
- convolve_in: bfloat16 [2, 512, 1024], P('pipe', 'dp'), may hold values from -0.25 to 0.25
- convolve_depth: bfloat16 [2, 15, 512], P('pipe', None, 'dp'), may hold values from -1.5 to 1.5
- convolve_norm: bfloat16 [2, 512], P('pipe', 'dp'), may hold values from 0.25 to 1.75
- convolve_out: bfloat16 [2, 512, 512], P('pipe', 'dp'), may hold values from -0.25 to 0.25
- late_gain: bfloat16 [2, 512], P('pipe', 'dp'), may hold values from 0.25 to 1.75
- late_up: bfloat16 [2, 512, 2048], P('pipe', 'dp'), may hold values from -0.25 to 0.25
- late_down: bfloat16 [2, 2048, 512], P('pipe', None, 'dp'), may hold values from -0.125 to 0.125
- final_gain: bfloat16 [2, 512], P('pipe', 'dp'), may hold values from 0.25 to 1.75
Outputs:
- layer_outputs: bfloat16 [2, 2, 16, 384, 512], P('pipe', None, 'dp')
- input_grads: bfloat16 [2, 2, 16, 384, 512], P('pipe', None, 'dp')
- grad_early_gain: float32 [2, 512], P('pipe', 'dp')
- grad_early_up: float32 [2, 512, 2048], P('pipe', 'dp')
- grad_early_down: float32 [2, 2048, 512], P('pipe', None, 'dp')
- grad_attend_gain: float32 [2, 512], P('pipe', 'dp')
- grad_attend_proj: float32 [2, 512, 1536], P('pipe', 'dp')
- grad_attend_out: float32 [2, 512, 512], P('pipe', 'dp')
- grad_convolve_gain: float32 [2, 512], P('pipe', 'dp')
- grad_convolve_in: float32 [2, 512, 1024], P('pipe', 'dp')
- grad_convolve_depth: float32 [2, 15, 512], P('pipe', None, 'dp')
- grad_convolve_norm: float32 [2, 512], P('pipe', 'dp')
- grad_convolve_out: float32 [2, 512, 512], P('pipe', 'dp')
- grad_late_gain: float32 [2, 512], P('pipe', 'dp')
- grad_late_up: float32 [2, 512, 2048], P('pipe', 'dp')
- grad_late_down: float32 [2, 2048, 512], P('pipe', None, 'dp')
- grad_final_gain: float32 [2, 512], P('pipe', 'dp')
Inputs may be any that keep to these rules, and one draw needn't show every extreme that they name: micro-batch 0 holds lengths from 96 to 192, the others from 192 to 384; the shortest length, 96, and the longest, 384, occur in every draw.
All inputs are finite; a program needn't handle non-finite values. No bound on the sum of `stream_flags` on one device may be relied on, other than what follows from the above.
Results may differ from a plain program's by a relative error of at most 0.023.
Values may be sent and summed in bfloat16 or wider, within the bound.
A program may use at most 256 MiB of HBM per device.

v0:
```python
import math

import jax
import jax.numpy as jnp
from jax import lax
from jax.sharding import PartitionSpec as P

HEADS = 8
KERNEL = 15


EPSILON = 1e-05


def shifted(block, axis, distance):
    devices = range(lax.axis_size(axis))
    route = [(i - distance, i) for i in devices if i - distance in devices]
    return lax.ppermute(block, axis, route)


def layer_norm(values, scales):
    center = values - jnp.mean(values, axis=-1, keepdims=True)
    spread = jnp.mean(center * center, axis=-1, keepdims=True)
    return center * lax.rsqrt(spread + EPSILON) * scales


def rotary_tables(frame_count, head_size):
    half_size = head_size // 2
    rates = jnp.exp(
        jnp.arange(half_size).astype(jnp.float32) * (-2.0 * math.log(10000.0) / head_size)
    )
    phases = jnp.arange(frame_count).astype(jnp.float32)[:, None] * rates[None, :]
    return (jnp.cos(phases)[:, None, :], jnp.sin(phases)[:, None, :])


def rotate(values, cosine, sine_table):
    half_size = values.shape[-1] // 2
    front = values[..., :half_size]
    behind = values[..., half_size:]
    return jnp.concatenate(
        [front * cosine - behind * sine_table, front * sine_table + behind * cosine], axis=-1
    )


def forward_product(left, right):
    return jnp.einsum("ulk,kn->uln", left, right, preferred_element_type=jnp.float32)


def weight_product(left, grads):
    return jnp.einsum("ulk,uln->kn", left, grads, preferred_element_type=jnp.float32)


def back_product(grads, right):
    return jnp.einsum("uln,kn->ulk", grads, right, preferred_element_type=jnp.float32)


def micro_masks(lengths, stream_flags, span_sizes, position, frame_count):
    length = lax.dynamic_index_in_dim(lengths, position, 0, keepdims=False)
    stream_flag = lax.dynamic_index_in_dim(stream_flags, position, 0, keepdims=False)
    span_size = lax.dynamic_index_in_dim(span_sizes, position, 0, keepdims=False)
    places = jnp.arange(frame_count, dtype=jnp.int32)
    query_block = places[None, :, None] // span_size[:, None, None]
    key_block = places[None, None, :] // span_size[:, None, None]
    visible = (places[None, None, :] < length[:, None, None]) & (
        (stream_flag[:, None, None] == 0) | (key_block <= query_block)
    )
    live_rows = (places[None, :] < length[:, None]).astype(jnp.float32)[:, :, None]
    tap_index = jnp.arange(KERNEL, dtype=jnp.int32)
    tap_live = ((stream_flag[:, None] == 0) | (tap_index[None, :] <= KERNEL // 2)).astype(
        jnp.float32
    )
    return (visible, live_rows, tap_live)


def convolve_tail(gates, depth_taps, norm_scales, live_rows, tap_live):
    channels = gates.shape[-1] // 2
    frame_count = gates.shape[1]
    glu_out = gates[..., :channels] * jax.nn.sigmoid(gates[..., channels:]) * live_rows
    padded = jnp.pad(glu_out, ((0, 0), (KERNEL // 2, KERNEL // 2), (0, 0)))
    mixed = jnp.zeros_like(glu_out)
    for offset in range(KERNEL):
        tap_weight = depth_taps[offset][None, None, :] * tap_live[:, offset][:, None, None]
        mixed = mixed + tap_weight * padded[:, offset : offset + frame_count]
    return jax.nn.silu(layer_norm(mixed, norm_scales))


def attend_forward(normed, projection, visible):
    batch_count, frame_count, _ = normed.shape
    projected = forward_product(normed, projection)
    channels = projected.shape[-1] // 3
    head_size = channels // HEADS
    split_heads = projected.reshape(batch_count, frame_count, 3, HEADS, head_size)
    cosine, sine_table = rotary_tables(frame_count, head_size)
    queries = rotate(split_heads[:, :, 0], cosine, sine_table).astype(jnp.bfloat16)
    key_rows = rotate(split_heads[:, :, 1], cosine, sine_table).astype(jnp.bfloat16)
    value_rows = split_heads[:, :, 2].astype(jnp.bfloat16)
    scores = jnp.einsum(
        "uihd,ujhd->uhij", queries, key_rows, preferred_element_type=jnp.float32
    ) * head_size ** (-0.5)
    scores = jnp.where(visible[:, None], scores, -1e30)
    powers = jnp.exp(scores - jnp.max(scores, axis=-1, keepdims=True))
    soft_weights = powers / jnp.sum(powers, axis=-1, keepdims=True)
    soft_low = soft_weights.astype(jnp.bfloat16)
    context = jnp.einsum(
        "uhij,ujhd->uihd", soft_low, value_rows, preferred_element_type=jnp.float32
    )
    context = context.astype(jnp.bfloat16).reshape(batch_count, frame_count, channels)
    return (context, (queries, key_rows, value_rows, soft_weights, soft_low, cosine, sine_table))


def layer_forward(stream, full, masks):
    (
        early_gain,
        early_up,
        early_down,
        attend_gain,
        attend_proj,
        attend_out,
        convolve_gain,
        convolve_in,
        convolve_depth,
        convolve_norm,
        convolve_out,
        late_gain,
        late_up,
        late_down,
        final_gain,
    ) = full
    visible, live_rows, tap_live = masks
    early_normed = layer_norm(stream, early_gain.astype(jnp.float32)).astype(jnp.bfloat16)
    early_inner = forward_product(early_normed, early_up)
    early_hidden = jax.nn.silu(early_inner).astype(jnp.bfloat16)
    after_early = stream + 0.5 * forward_product(early_hidden, early_down)
    attend_normed = layer_norm(after_early, attend_gain.astype(jnp.float32)).astype(jnp.bfloat16)
    context, attend_saved = attend_forward(attend_normed, attend_proj, visible)
    after_attend = after_early + forward_product(context, attend_out)
    convolve_normed = layer_norm(after_attend, convolve_gain.astype(jnp.float32)).astype(
        jnp.bfloat16
    )
    gates = forward_product(convolve_normed, convolve_in)
    convolve_hidden = convolve_tail(
        gates,
        convolve_depth.astype(jnp.float32),
        convolve_norm.astype(jnp.float32),
        live_rows,
        tap_live,
    ).astype(jnp.bfloat16)
    after_convolve = after_attend + forward_product(convolve_hidden, convolve_out)
    late_normed = layer_norm(after_convolve, late_gain.astype(jnp.float32)).astype(jnp.bfloat16)
    late_inner = forward_product(late_normed, late_up)
    late_hidden = jax.nn.silu(late_inner).astype(jnp.bfloat16)
    after_late = after_convolve + 0.5 * forward_product(late_hidden, late_down)
    result = layer_norm(after_late, final_gain.astype(jnp.float32))
    saved = (
        after_early,
        after_attend,
        after_convolve,
        after_late,
        early_normed,
        early_inner,
        early_hidden,
        attend_normed,
        context,
        attend_saved,
        convolve_normed,
        gates,
        convolve_hidden,
        late_normed,
        late_inner,
        late_hidden,
    )
    return (result, saved)


def feed_back(stream_grad, stream_in, scales, up_matrix, down_matrix, normed, inner, hidden):
    branch_grad = (0.5 * stream_grad).astype(jnp.bfloat16)
    down_grad = weight_product(hidden, branch_grad)
    hidden_grad = back_product(branch_grad, down_matrix)
    inner_back = jax.vjp(jax.nn.silu, inner)[1]
    inner_grad = inner_back(hidden_grad)[0].astype(jnp.bfloat16)
    up_grad = weight_product(normed, inner_grad)
    normed_grad = back_product(inner_grad, up_matrix)
    norm_back = jax.vjp(layer_norm, stream_in, scales.astype(jnp.float32))[1]
    input_grad, scale_grad = norm_back(normed_grad)
    return (stream_grad + input_grad, (scale_grad, up_grad, down_grad))


def attend_back(
    stream_grad, stream_in, scales, projection, out_matrix, normed, context, attend_saved
):
    queries, key_rows, value_rows, soft_weights, soft_low, cosine, sine_table = attend_saved
    batch_count, frame_count, channels = context.shape
    head_size = channels // HEADS
    branch_grad = stream_grad.astype(jnp.bfloat16)
    out_grad = weight_product(context, branch_grad)
    context_grad = back_product(branch_grad, out_matrix).astype(jnp.bfloat16)
    context_grad = context_grad.reshape(batch_count, frame_count, HEADS, head_size)
    soft_grad = jnp.einsum(
        "uihd,ujhd->uhij", context_grad, value_rows, preferred_element_type=jnp.float32
    )
    value_grad = jnp.einsum(
        "uhij,uihd->ujhd", soft_low, context_grad, preferred_element_type=jnp.float32
    )
    score_grad = soft_weights * (
        soft_grad - jnp.sum(soft_grad * soft_weights, axis=-1, keepdims=True)
    )
    score_grad = score_grad.astype(jnp.bfloat16)
    query_grad = jnp.einsum(
        "uhij,ujhd->uihd", score_grad, key_rows, preferred_element_type=jnp.float32
    ) * head_size ** (-0.5)
    key_grad = jnp.einsum(
        "uhij,uihd->ujhd", score_grad, queries, preferred_element_type=jnp.float32
    ) * head_size ** (-0.5)
    query_grad = rotate(query_grad, cosine, -sine_table)
    key_grad = rotate(key_grad, cosine, -sine_table)
    projected_grad = jnp.stack([query_grad, key_grad, value_grad], axis=2)
    projected_grad = projected_grad.reshape(batch_count, frame_count, 3 * channels).astype(
        jnp.bfloat16
    )
    projection_grad = weight_product(normed, projected_grad)
    normed_grad = back_product(projected_grad, projection)
    norm_back = jax.vjp(layer_norm, stream_in, scales.astype(jnp.float32))[1]
    input_grad, scale_grad = norm_back(normed_grad)
    return (stream_grad + input_grad, (scale_grad, projection_grad, out_grad))


def convolve_back(stream_grad, stream_in, full, masks, normed, gates, hidden):
    convolve_gain, convolve_in, convolve_depth, convolve_norm, convolve_out = full
    visible, live_rows, tap_live = masks
    branch_grad = stream_grad.astype(jnp.bfloat16)
    out_grad = weight_product(hidden, branch_grad)
    hidden_grad = back_product(branch_grad, convolve_out)

    def tail_only(gate_values, depth_taps, norm_scales):
        return convolve_tail(gate_values, depth_taps, norm_scales, live_rows, tap_live)

    tail_back = jax.vjp(
        tail_only, gates, convolve_depth.astype(jnp.float32), convolve_norm.astype(jnp.float32)
    )[1]
    gates_grad, depth_grad, mid_grad = tail_back(hidden_grad)
    gates_grad = gates_grad.astype(jnp.bfloat16)
    in_grad = weight_product(normed, gates_grad)
    normed_grad = back_product(gates_grad, convolve_in)
    norm_back = jax.vjp(layer_norm, stream_in, convolve_gain.astype(jnp.float32))[1]
    input_grad, scale_grad = norm_back(normed_grad)
    return (stream_grad + input_grad, (scale_grad, in_grad, depth_grad, mid_grad, out_grad))


def layer_backward(stream, full, masks, output_grad):
    (
        early_gain,
        early_up,
        early_down,
        attend_gain,
        attend_proj,
        attend_out,
        convolve_gain,
        convolve_in,
        convolve_depth,
        convolve_norm,
        convolve_out,
        late_gain,
        late_up,
        late_down,
        final_gain,
    ) = full
    _, saved = layer_forward(stream, full, masks)
    (
        after_early,
        after_attend,
        after_convolve,
        after_late,
        early_normed,
        early_inner,
        early_hidden,
        attend_normed,
        context,
        attend_saved,
        convolve_normed,
        gates,
        convolve_hidden,
        late_normed,
        late_inner,
        late_hidden,
    ) = saved
    final_back = jax.vjp(layer_norm, after_late, final_gain.astype(jnp.float32))[1]
    stream_grad, final_grad = final_back(output_grad)
    stream_grad, late_grads = feed_back(
        stream_grad,
        after_convolve,
        late_gain,
        late_up,
        late_down,
        late_normed,
        late_inner,
        late_hidden,
    )
    stream_grad, convolve_grads = convolve_back(
        stream_grad,
        after_attend,
        (convolve_gain, convolve_in, convolve_depth, convolve_norm, convolve_out),
        masks,
        convolve_normed,
        gates,
        convolve_hidden,
    )
    stream_grad, attend_grads = attend_back(
        stream_grad,
        after_early,
        attend_gain,
        attend_proj,
        attend_out,
        attend_normed,
        context,
        attend_saved,
    )
    stream_grad, early_grads = feed_back(
        stream_grad,
        stream,
        early_gain,
        early_up,
        early_down,
        early_normed,
        early_inner,
        early_hidden,
    )
    return (stream_grad, early_grads + attend_grads + convolve_grads + late_grads + (final_grad,))


def fetch_once(shards):
    gathered = (
        lax.all_gather(shards[0], "dp", axis=1, tiled=True),
        lax.all_gather(shards[1], "dp", axis=1, tiled=True),
        lax.all_gather(shards[2], "dp", axis=2, tiled=True),
        lax.all_gather(shards[3], "dp", axis=1, tiled=True),
        lax.all_gather(shards[4], "dp", axis=1, tiled=True),
        lax.all_gather(shards[5], "dp", axis=1, tiled=True),
        lax.all_gather(shards[6], "dp", axis=1, tiled=True),
        lax.all_gather(shards[7], "dp", axis=1, tiled=True),
        lax.all_gather(shards[8], "dp", axis=2, tiled=True),
        lax.all_gather(shards[9], "dp", axis=1, tiled=True),
        lax.all_gather(shards[10], "dp", axis=1, tiled=True),
        lax.all_gather(shards[11], "dp", axis=1, tiled=True),
        lax.all_gather(shards[12], "dp", axis=1, tiled=True),
        lax.all_gather(shards[13], "dp", axis=2, tiled=True),
        lax.all_gather(shards[14], "dp", axis=1, tiled=True),
    )
    return tuple((piece[0] for piece in gathered))


def body(
    frames,
    cotangent,
    lengths,
    stream_flags,
    span_sizes,
    early_gain,
    early_up,
    early_down,
    attend_gain,
    attend_proj,
    attend_out,
    convolve_gain,
    convolve_in,
    convolve_depth,
    convolve_norm,
    convolve_out,
    late_gain,
    late_up,
    late_down,
    final_gain,
):
    shards = (
        early_gain,
        early_up,
        early_down,
        attend_gain,
        attend_proj,
        attend_out,
        convolve_gain,
        convolve_in,
        convolve_depth,
        convolve_norm,
        convolve_out,
        late_gain,
        late_up,
        late_down,
        final_gain,
    )
    section = lax.axis_index("pipe")
    micro_count = frames.shape[0]
    frame_count = frames.shape[2]
    full = None
    full = fetch_once(shards)
    received = jnp.zeros(frames.shape[1:], jnp.bfloat16)
    outputs = jnp.zeros(frames.shape, jnp.bfloat16)
    inputs_kept = jnp.zeros(frames.shape, jnp.bfloat16)
    for tick in range(micro_count + 1):
        index_now = tick - section
        valid = (index_now >= 0) & (index_now < micro_count)
        position = jnp.clip(index_now, 0, micro_count - 1)
        incoming = jnp.where(section == 0, frames[min(tick, micro_count - 1)], received)
        masks = micro_masks(lengths, stream_flags, span_sizes, position, frame_count)

        def forward_run(layer_in):
            return layer_forward(layer_in.astype(jnp.float32), full, masks)[0].astype(jnp.bfloat16)

        def forward_skip(layer_in):
            return jnp.zeros_like(layer_in)

        result = lax.cond(valid, forward_run, forward_skip, incoming)
        outputs = jnp.where(
            valid, lax.dynamic_update_index_in_dim(outputs, result, position, 0), outputs
        )
        inputs_kept = jnp.where(
            valid, lax.dynamic_update_index_in_dim(inputs_kept, incoming, position, 0), inputs_kept
        )
        if tick < micro_count:
            received = shifted(result, "pipe", 1)
    returned = jnp.zeros(frames.shape[1:], jnp.bfloat16)
    input_grads = jnp.zeros(frames.shape, jnp.bfloat16)
    gathered_dims = (0, 0, 1, 0, 0, 0, 0, 0, 1, 0, 0, 0, 0, 1, 0)
    widths = lax.axis_size("dp")
    totals = tuple(
        (
            jnp.zeros(
                tuple(
                    (
                        size * widths if axis == dim else size
                        for axis, size in enumerate(piece.shape[1:])
                    )
                ),
                jnp.float32,
            )
            for piece, dim in zip(shards, gathered_dims)
        )
    )
    for tick in range(micro_count + 1):
        index_now = tick - (1 - section)
        valid = (index_now >= 0) & (index_now < micro_count)
        position = jnp.clip(index_now, 0, micro_count - 1)
        seed_grad = jnp.where(section == 1, cotangent[min(tick, micro_count - 1)], returned)
        layer_in = lax.dynamic_index_in_dim(inputs_kept, position, 0, keepdims=False)
        masks = micro_masks(lengths, stream_flags, span_sizes, position, frame_count)

        def backward_run(stream_in, grad_in, running):
            input_grad, weight_grads = layer_backward(
                stream_in.astype(jnp.float32), full, masks, grad_in.astype(jnp.float32)
            )
            return (input_grad.astype(jnp.bfloat16), jax.tree.map(jnp.add, running, weight_grads))

        def backward_skip(stream_in, grad_in, running):
            return (jnp.zeros_like(stream_in), running)

        input_grad, totals = lax.cond(
            valid, backward_run, backward_skip, layer_in, seed_grad, totals
        )
        input_grads = jnp.where(
            valid,
            lax.dynamic_update_index_in_dim(input_grads, input_grad, position, 0),
            input_grads,
        )
        if tick < micro_count:
            returned = shifted(input_grad, "pipe", -1)
    summed = (
        lax.psum_scatter(totals[0][None], "dp", scatter_dimension=1, tiled=True),
        lax.psum_scatter(totals[1][None], "dp", scatter_dimension=1, tiled=True),
        lax.psum_scatter(totals[2][None], "dp", scatter_dimension=2, tiled=True),
        lax.psum_scatter(totals[3][None], "dp", scatter_dimension=1, tiled=True),
        lax.psum_scatter(totals[4][None], "dp", scatter_dimension=1, tiled=True),
        lax.psum_scatter(totals[5][None], "dp", scatter_dimension=1, tiled=True),
        lax.psum_scatter(totals[6][None], "dp", scatter_dimension=1, tiled=True),
        lax.psum_scatter(totals[7][None], "dp", scatter_dimension=1, tiled=True),
        lax.psum_scatter(totals[8][None], "dp", scatter_dimension=2, tiled=True),
        lax.psum_scatter(totals[9][None], "dp", scatter_dimension=1, tiled=True),
        lax.psum_scatter(totals[10][None], "dp", scatter_dimension=1, tiled=True),
        lax.psum_scatter(totals[11][None], "dp", scatter_dimension=1, tiled=True),
        lax.psum_scatter(totals[12][None], "dp", scatter_dimension=1, tiled=True),
        lax.psum_scatter(totals[13][None], "dp", scatter_dimension=2, tiled=True),
        lax.psum_scatter(totals[14][None], "dp", scatter_dimension=1, tiled=True),
    )
    return (outputs[None], input_grads[None]) + tuple(summed)


def solution(mesh):
    return jax.shard_map(
        body,
        mesh=mesh,
        in_specs=(
            P(None, "dp", None, None),
            P(None, "dp", None, None),
            P(None, "dp"),
            P(None, "dp"),
            P(None, "dp"),
            P("pipe", "dp"),
            P("pipe", "dp", None),
            P("pipe", None, "dp"),
            P("pipe", "dp"),
            P("pipe", "dp", None),
            P("pipe", "dp", None),
            P("pipe", "dp"),
            P("pipe", "dp", None),
            P("pipe", None, "dp"),
            P("pipe", "dp"),
            P("pipe", "dp", None),
            P("pipe", "dp"),
            P("pipe", "dp", None),
            P("pipe", None, "dp"),
            P("pipe", "dp"),
        ),
        out_specs=(
            P("pipe", None, "dp", None, None),
            P("pipe", None, "dp", None, None),
            P("pipe", "dp"),
            P("pipe", "dp", None),
            P("pipe", None, "dp"),
            P("pipe", "dp"),
            P("pipe", "dp", None),
            P("pipe", "dp", None),
            P("pipe", "dp"),
            P("pipe", "dp", None),
            P("pipe", None, "dp"),
            P("pipe", "dp"),
            P("pipe", "dp", None),
            P("pipe", "dp"),
            P("pipe", "dp", None),
            P("pipe", None, "dp"),
            P("pipe", "dp"),
        ),
        check_vma=False,
    )
```

profile of v0, /device:TPU:0, one launch (start us, length us, event | category | flops | bytes accessed | tf_op | source)
XLA Modules:
  0.0 1797.8 jit_solution(3335298209672392180)
XLA Ops:
  19.8 24.0 %all_gather.51 = bf16[1,15,512]{1,0,2:T(2,128)(2,1)S(1)} all-gather(bf16[1,15,32]{1,0,2:T(2,128)(2,1)S(1)} %copy.177), channel_id=1, replica_groups=mesh['pipe'=2,'dp'=16] {'dp'}, dimensions={2}, use_global_device_ids=true | all-gather | bytes 16320 | tf_op jit(solution)/shard_map/all_gather | solution.py:340
  50.9 31.2 %all-reduce.108 = (bf16[512]{0:T(512)(128)(2,1)}, bf16[512]{0:T(512)(128)(2,1)}, bf16[512]{0:T(512)(128)(2,1)}, bf16[512]{0:T(512)(128)(2,1)}, bf16[512]{0:T(512)(128)(2,1)}, /*index=5*/bf16[512]{0:T(512)(128)(2,1)}) all-reduce(bf16[512]{0:T(512)(128)(2,1)S(1)} %dynamic-update-slice.11, ...), channel_id=1, replica_groups=mesh['pipe'=2,'dp'=16] {'dp'}, use_global_device_ids=true, to_apply=%add.102 | all-reduce | flops 3072 | bytes 12288 | tf_op jit(solution)/shard_map/squeeze | solution.py:348
  88.0 19.0 %all_gather.50 = bf16[1,512,512]{2,1,0:T(8,128)(2,1)S(1)} all-gather(bf16[1,32,512]{2,1,0:T(8,128)(2,1)} %param.46), channel_id=1, replica_groups=mesh['pipe'=2,'dp'=16] {'dp'}, dimensions={1}, use_global_device_ids=true | all-gather | bytes 557056 | tf_op jit(solution)/shard_map/all_gather | solution.py:337
  107.0 23.3 %all_gather.55 = bf16[1,512,512]{2,1,0:T(8,128)(2,1)} all-gather(bf16[1,32,512]{2,1,0:T(8,128)(2,1)} %param.51), channel_id=1, replica_groups=mesh['pipe'=2,'dp'=16] {'dp'}, dimensions={1}, use_global_device_ids=true | all-gather | bytes 557056 | tf_op jit(solution)/shard_map/all_gather | solution.py:342
  130.5 5.3 all-gather.7.cloned.1.call-done
  135.8 42.5 %all-gather.9.cloned.1.call-done = bf16[1,2048,512]{1,2,0:T(8,128)(2,1)} async-done(((bf16[1,2048,32]{1,2,0:T(8,128)(2,1)}), bf16[1,2048,512]{1,2,0:T(8,128)(2,1)}) %all-gather.9.cloned.1.call-update) | async-done | bytes 2097168 | tf_op jit(solution)/shard_map/all_gather | solution.py:334
  178.3 42.2 %all-gather.15.cloned.1.call-done = bf16[1,512,2048]{2,1,0:T(8,128)(2,1)} async-done(((bf16[1,32,2048]{2,1,0:T(8,128)(2,1)}), bf16[1,512,2048]{2,1,0:T(8,128)(2,1)}) %all-gather.15.cloned.1.call-update) | async-done | bytes 2097168 | tf_op jit(solution)/shard_map/all_gather | solution.py:344
  220.5 42.2 %all-gather.17.cloned.1.call-done = bf16[1,2048,512]{1,2,0:T(8,128)(2,1)} async-done(((bf16[1,2048,32]{1,2,0:T(8,128)(2,1)}), bf16[1,2048,512]{1,2,0:T(8,128)(2,1)}) %all-gather.17.cloned.1.call-update) | async-done | bytes 2097168 | tf_op jit(solution)/shard_map/all_gather | solution.py:345
  264.9 62.6 %conditional.6 = (bf16[1,384,512]{2,1,0:T(8,128)(2,1)S(1)}, bf16[1,1,384,512]{3,2,1,0:T(8,128)(2,1)}) conditional(s32[]{:T(128)} %convert_element_type.1349, () %tuple.85, (bf16[1,1,384,512]{3,2,1,0:T(8,128)(2,1)S(1)}, pred[1,384,512]{2,1,0:T(8,128)(4,1)S(1)}, bf16[1,384,512]{2,1,0:T(8,128)(2,1)}, bf16[512]{0:T(512)(128)(2,1)}, ...), branch_computations={%region_0.3_spmd, %region_1.18_spmd} | conditional | flops 4971124736 | bytes 94762568 | solution.py:411
  277.2 4.4 slice_multiply_fusion.13
  281.6 6.4 slice_multiply_fusion.14
  291.3 5.2 fusion.660
  304.8 3.8 fusion.663
  317.7 4.8 fusion.666
  331.1 6.7 collective-permute-done
  339.8 55.0 %conditional.7 = (bf16[1,384,512]{2,1,0:T(8,128)(2,1)S(1)}, bf16[1,1,384,512]{3,2,1,0:T(8,128)(2,1)}) conditional(s32[]{:T(128)} %convert_element_type.1352, () %tuple.87, (bf16[1,384,512]{2,1,0:T(8,128)(2,1)S(1)}, bf16[512]{0:T(512)(128)(2,1)}, bf16[512,2048]{1,0:T(8,128)(2,1)}, bf16[2048,512]{0,1:T(8,128)(2,1)}, bf16[512]{0:T(512)(128)(2,1)}, ...), branch_computations={%region_16.19_spmd, %region_17.34_spmd} | conditional | flops 4970928128 | bytes 92830664 | solution.py:411
  348.4 5.2 fusion.670
  355.6 3.9 slice_multiply_fusion.28
  359.6 5.9 slice_multiply_fusion.29
  372.5 3.8 fusion.673
  385.2 4.8 fusion.676
  394.8 4.2 collective-permute-start.1
  401.2 6.0 collective-permute-done.1
  409.9 36.4 %conditional.9 = (bf16[1,384,512]{2,1,0:T(8,128)(2,1)}, f32[512]{0:T(512)}, f32[512,2048]{1,0:T(8,128)}, f32[2048,512]{1,0:T(8,128)}, f32[512]{0:T(512)}, /*inde...) conditional(s32[]{:T(128)} %convert_element_type.1358, ...), branch_computations={%region_48.51_spmd, %region_49.100_spmd} | conditional | flops 14921831424 | bytes 382622976 | solution.py:455
  451.9 88.7 %collective-permute-done.2 = bf16[1,384,512]{2,1,0:T(8,128)(2,1)} collective-permute-done((bf16[1,384,512]{2,1,0:T(8,128)(2,1)}, bf16[1,384,512]{2,1,0:T(8,128)(2,1)}, u32[]{:S(2)}, u32[]{:S(2)}) %collective-permute-start.2) | collective-permute-done | bytes 393248 | tf_op jit(solution)/shard_map/ppermute | solution.py:18
  541.2 138.4 %conditional.10 = (bf16[1,384,512]{2,1,0:T(8,128)(2,1)}, f32[512]{0:T(512)}, f32[512,2048]{1,0:T(8,128)}, f32[2048,512]{1,0:T(8,128)}, f32[512]{0:T(512)}, /*ind...) conditional(s32[]{:T(128)} %convert_element_type.1361, ...), branch_computations={%region_98.101_spmd, %region_99.150_spmd} | conditional | flops 14927874048 | bytes 403748704 | solution.py:455
  552.4 4.5 slice_multiply_fusion.73
  556.9 6.3 slice_multiply_fusion.74
  575.9 3.8 fusion.697
  596.4 5.7 convolution_add_fusion.3
  603.2 5.6 convolution_add_fusion.4
  631.7 3.8 convolution_add_fusion.7
  653.5 4.9 convolution_add_fusion.2
  662.5 5.8 convolution_add_fusion.5
  669.3 5.7 convolution_add_fusion.6
  683.1 7.9 collective-permute-done.3
  691.7 136.5 %conditional.11 = (f32[512]{0:T(512)}, f32[512,2048]{1,0:T(8,128)}, f32[2048,512]{1,0:T(8,128)}, f32[512]{0:T(512)}, f32[512,1536]{1,0:T(8,128)}, /*index=5*/f32...) conditional(s32[]{:T(128)} %convert_element_type.1364, ...), branch_computations={%region_148.151_spmd, %region_149.200_spmd} | conditional | flops 14927873024 | bytes 401340192 | solution.py:455
  703.0 4.5 slice_multiply_fusion.88
  707.5 6.4 slice_multiply_fusion.89
  726.7 3.9 fusion.703
  747.3 5.7 convolution_add_fusion.13
  754.1 5.6 convolution_add_fusion.14
  782.9 3.8 convolution_add_fusion.17
  803.9 4.9 convolution_add_fusion.12
  812.6 5.8 convolution_add_fusion.15
  819.5 5.7 convolution_add_fusion.16
  841.3 4.1 bitcast_reduce_fusion
  849.1 5.4 copy.204
  854.6 5.5 copy.205
  877.8 5.3 reduce-scatter.46.cloned.1.call-done
  884.4 56.6 %reduce-scatter.48.cloned.1.call-done = f32[32,1]{1,0:T(8,128)} async-done(((f32[512,1]{1,0:T(8,128)}), f32[32,1]{1,0:T(8,128)}) %reduce-scatter.48.cloned.1.call-update) | async-done | bytes 144
  942.3 56.6 %reduce-scatter.50.cloned.1.call-done = f32[32,1]{1,0:T(8,128)} async-done(((f32[512,1]{1,0:T(8,128)}), f32[32,1]{1,0:T(8,128)}) %reduce-scatter.50.cloned.1.call-update) | async-done | bytes 144
  1000.1 56.4 %reduce-scatter.54.cloned.1.call-done = f32[32,1]{1,0:T(8,128)} async-done(((f32[512,1]{1,0:T(8,128)}), f32[32,1]{1,0:T(8,128)}) %reduce-scatter.54.cloned.1.call-update) | async-done | bytes 144
  1057.9 56.6 %reduce-scatter.56.cloned.1.call-done = f32[32,1]{1,0:T(8,128)} async-done(((f32[512,1]{1,0:T(8,128)}), f32[32,1]{1,0:T(8,128)}) %reduce-scatter.56.cloned.1.call-update) | async-done | bytes 144
  1115.8 56.4 %reduce-scatter.58.cloned.1.call-done = f32[32,1]{1,0:T(8,128)} async-done(((f32[512,1]{1,0:T(8,128)}), f32[32,1]{1,0:T(8,128)}) %reduce-scatter.58.cloned.1.call-update) | async-done | bytes 144
  1173.5 56.6 %reduce-scatter.52.cloned.1.call-done = f32[32,15]{1,0:T(8,128)} async-done(((f32[512,15]{1,0:T(8,128)}), f32[32,15]{1,0:T(8,128)}) %reduce-scatter.52.cloned.1.call-update) | async-done | bytes 1936
  1231.7 58.9 %reduce-scatter.36.cloned.1.call-done = f32[1,32,512]{2,1,0:T(8,128)} async-done(((f32[1,512,512]{2,1,0:T(8,128)}), f32[1,32,512]{2,1,0:T(8,128)}) %reduce-scatter.36.cloned.1.call-update) | async-done | bytes 65552 | tf_op jit(solution)/shard_map/reduce_scatter | solution.py:471
  1290.7 60.9 %reduce-scatter.40.cloned.1.call-done = f32[1,32,512]{2,1,0:T(8,128)} async-done(((f32[1,512,512]{2,1,0:T(8,128)}), f32[1,32,512]{2,1,0:T(8,128)}) %reduce-scatter.40.cloned.1.call-update) | async-done | bytes 65552 | tf_op jit(solution)/shard_map/reduce_scatter | solution.py:476
  1351.6 64.8 %reduce-scatter.38.cloned.1.call-done = f32[1,32,1024]{2,1,0:T(8,128)} async-done(((f32[1,512,1024]{2,1,0:T(8,128)}), f32[1,32,1024]{2,1,0:T(8,128)}) %reduce-scatter.38.cloned.1.call-update) | async-done | bytes 131088 | tf_op jit(solution)/shard_map/reduce_scatter | solution.py:473
  1416.4 70.0 %reduce-scatter.34.cloned.1.call-done = f32[1,32,1536]{2,1,0:T(8,128)} async-done(((f32[1,512,1536]{2,1,0:T(8,128)}), f32[1,32,1536]{2,1,0:T(8,128)}) %reduce-scatter.34.cloned.1.call-update) | async-done | bytes 196624 | tf_op jit(solution)/shard_map/reduce_scatter | solution.py:470
  1486.4 76.2 %reduce-scatter.30.cloned.1.call-done = f32[1,32,2048]{2,1,0:T(8,128)} async-done(((f32[1,512,2048]{2,1,0:T(8,128)}), f32[1,32,2048]{2,1,0:T(8,128)}) %reduce-scatter.30.cloned.1.call-update) | async-done | bytes 262160 | tf_op jit(solution)/shard_map/reduce_scatter | solution.py:467
  1562.5 75.9 %reduce-scatter.42.cloned.1.call-done = f32[1,32,2048]{2,1,0:T(8,128)} async-done(((f32[1,512,2048]{2,1,0:T(8,128)}), f32[1,32,2048]{2,1,0:T(8,128)}) %reduce-scatter.42.cloned.1.call-update) | async-done | bytes 262160 | tf_op jit(solution)/shard_map/reduce_scatter | solution.py:478
  1638.4 76.3 %reduce-scatter.32.cloned.1.call-done = f32[1,2048,32]{1,2,0:T(8,128)} async-done(((f32[1,2048,512]{1,2,0:T(8,128)}), f32[1,2048,32]{1,2,0:T(8,128)}) %reduce-scatter.32.cloned.1.call-update) | async-done | bytes 262160 | tf_op jit(solution)/shard_map/reduce_scatter | solution.py:468
  1714.7 75.9 %reduce-scatter.44.cloned.1.call-done = f32[1,2048,32]{1,2,0:T(8,128)} async-done(((f32[1,2048,512]{1,2,0:T(8,128)}), f32[1,2048,32]{1,2,0:T(8,128)}) %reduce-scatter.44.cloned.1.call-update) | async-done | bytes 262160 | tf_op jit(solution)/shard_map/reduce_scatter | solution.py:479
  (840 shorter events, 350.3 us)
Async XLA Ops:
  7.2 123.1 %copy-start.51 = (bf16[2,1,384,512]{3,2,1,0:T(8,128)(2,1)S(1)}, bf16[2,1,384,512]{3,2,1,0:T(8,128)(2,1)}, u32[]{:S(2)}) copy-start(bf16[2,1,384,512]{3,2,1,0:T(8,128)(2,1)} %param.36) | copy-start | bytes 2359300
  7.2 123.2 %all-gather.13.cloned.1.call-start = ((), (), s32[]{:S(2)}) async-start(), calls=%async_computation.18 | async-start | bytes 1114112 | tf_op jit(solution)/shard_map/all_gather | solution.py:339
  7.9 122.5 %all-gather.11.cloned.1.call-start = ((), (), s32[]{:S(2)}) async-start(), calls=%async_computation.17 | async-start | bytes 1671168 | tf_op jit(solution)/shard_map/all_gather | solution.py:336
  8.7 127.1 %all-gather.7.cloned.1.call-start = ((), (), s32[]{:S(2)}) async-start(), calls=%async_computation.15 | async-start | bytes 2228224 | tf_op jit(solution)/shard_map/all_gather | solution.py:333
  9.4 168.9 %all-gather.9.cloned.1.call-start = ((), (), s32[]{:S(2)}) async-start(), calls=%async_computation.16 | async-start | bytes 2228224 | tf_op jit(solution)/shard_map/all_gather | solution.py:334
  10.0 210.5 %all-gather.15.cloned.1.call-start = ((), (), s32[]{:S(2)}) async-start(), calls=%async_computation.19 | async-start | bytes 2228224 | tf_op jit(solution)/shard_map/all_gather | solution.py:344
  10.6 252.1 %all-gather.17.cloned.1.call-start = ((), (), s32[]{:S(2)}) async-start(), calls=%async_computation.20 | async-start | bytes 2228224 | tf_op jit(solution)/shard_map/all_gather | solution.py:345
  11.2 871.9 %reduce-scatter.46.cloned.1.call-start = ((), (), s32[]{:S(2)}) async-start(), calls=%async_computation.29 | async-start | bytes 278528
  107.0 584.7 %copy-start.6 = (bf16[1,512,512]{2,1,0:T(8,128)(2,1)}, bf16[1,512,512]{2,1,0:T(8,128)(2,1)S(1)}, u32[]{:S(2)}) copy-start(bf16[1,512,512]{2,1,0:T(8,128)(2,1)S(1)} %all_gather.50) | copy-start | bytes 1572868
  263.5 76.3 %copy-start.107 = (s32[1,384,1]{1,2,0:T(1,128)}, s32[1,384,1]{1,2,0:T(1,128)S(1)}, u32[]{:S(2)}) copy-start(s32[1,384,1]{1,2,0:T(1,128)S(1)} %ne.90) | copy-start | bytes 4612
  263.5 76.2 %copy-start.109 = (s32[1,1,384]{2,1,0:T(1,128)}, s32[1,1,384]{2,1,0:T(1,128)S(1)}, u32[]{:S(2)}) copy-start(s32[1,1,384]{2,1,0:T(1,128)S(1)} %ne.85) | copy-start | bytes 4612
  263.5 76.2 %copy-start.108 = (s32[1,384,1]{1,2,0:T(1,128)}, s32[1,384,1]{1,2,0:T(1,128)S(1)}, u32[]{:S(2)}) copy-start(s32[1,384,1]{1,2,0:T(1,128)S(1)} %broadcast.4305) | copy-start | bytes 4612
  327.5 10.4 collective-permute-start
  348.3 17.6 copy-start.2
  394.8 12.4 collective-permute-start.1
  446.3 94.3 %collective-permute-start.2 = (bf16[1,384,512]{2,1,0:T(8,128)(2,1)}, bf16[1,384,512]{2,1,0:T(8,128)(2,1)}, u32[]{:S(2)}, u32[]{:S(2)}) collective-permute-start(bf16[1,384,512]{2,1,0:T(8,128)(2,1)} %get-tuple-element.1080), channel_id=1, source_target_pairs={{16,0},{17,1},{18,2},{19,3},{20,4},{21,5},{22,6},{23,7},{24,8},{25... | collective-permute-start | bytes 1179656 | tf_op jit(solution)/shard_map/ppermute | solution.py:18
  541.2 27.1 %copy-start.16 = (bf16[512,2048]{1,0:T(8,128)(2,1)S(1)}, bf16[512,2048]{1,0:T(8,128)(2,1)}, u32[]{:S(2)}) copy-start(bf16[512,2048]{1,0:T(8,128)(2,1)} %get-tuple-element.897) | copy-start | bytes 6291460 | tf_op jit(solution)/shard_map/cond
  546.4 37.3 %copy-start.116 = (f32[512]{0:T(512)}, f32[512]{0:T(512)S(1)}, u32[]{:S(2)}) copy-start(f32[512]{0:T(512)S(1)} %convert_element_type.1230) | copy-start | bytes 6148 | tf_op jit(solution)/shard_map/cond
  547.1 24.7 %copy-start.121 = (f32[512]{0:T(512)}, f32[512]{0:T(512)S(1)}, u32[]{:S(2)}) copy-start(f32[512]{0:T(512)S(1)} %convert_element_type.1206) | copy-start | bytes 6148 | tf_op jit(solution)/shard_map/cond
  551.7 17.6 copy-start.186
  556.9 28.0 %copy-start.129 = (f32[1,512]{1,0:T(1,128)}, f32[1,512]{1,0:T(1,128)S(1)}, u32[]{:S(2)}) copy-start(f32[1,512]{1,0:T(1,128)S(1)} %get-tuple-element.2119) | copy-start | bytes 6148 | tf_op jit(solution)/shard_map/cond
  556.9 28.0 %copy-start.131 = (f32[1,512]{1,0:T(1,128)}, f32[1,512]{1,0:T(1,128)S(1)}, u32[]{:S(2)}) copy-start(f32[1,512]{1,0:T(1,128)S(1)} %get-tuple-element.2120) | copy-start | bytes 6148 | tf_op jit(solution)/shard_map/cond
  556.9 28.0 %copy-start.133 = (f32[1,512]{1,0:T(1,128)}, f32[1,512]{1,0:T(1,128)S(1)}, u32[]{:S(2)}) copy-start(f32[1,512]{1,0:T(1,128)S(1)} %get-tuple-element.2121) | copy-start | bytes 6148 | tf_op jit(solution)/shard_map/cond
  556.9 28.0 %copy-start.135 = (f32[1,512]{1,0:T(1,128)}, f32[1,512]{1,0:T(1,128)S(1)}, u32[]{:S(2)}) copy-start(f32[1,512]{1,0:T(1,128)S(1)} %get-tuple-element.2122) | copy-start | bytes 6148 | tf_op jit(solution)/shard_map/cond
  565.6 9.5 copy-start.87
  614.4 13.5 copy-start.130
  614.4 13.5 copy-start.132
  614.4 13.5 copy-start.134
  614.4 13.5 copy-start.136
  641.4 7.1 slice-start
  679.6 11.5 collective-permute-start.3
  691.7 27.4 %copy-start.18 = (bf16[512,2048]{1,0:T(8,128)(2,1)S(1)}, bf16[512,2048]{1,0:T(8,128)(2,1)}, u32[]{:S(2)}) copy-start(bf16[512,2048]{1,0:T(8,128)(2,1)} %get-tuple-element.955) | copy-start | bytes 6291460 | tf_op jit(solution)/shard_map/cond
  697.0 37.5 %copy-start.118 = (f32[512]{0:T(512)}, f32[512]{0:T(512)S(1)}, u32[]{:S(2)}) copy-start(f32[512]{0:T(512)S(1)} %convert_element_type.1297) | copy-start | bytes 6148 | tf_op jit(solution)/shard_map/cond
  697.7 25.0 %copy-start.123 = (f32[512]{0:T(512)}, f32[512]{0:T(512)S(1)}, u32[]{:S(2)}) copy-start(f32[512]{0:T(512)S(1)} %convert_element_type.1273) | copy-start | bytes 6148 | tf_op jit(solution)/shard_map/cond
  702.2 18.0 copy-start.188
  707.5 28.3 %copy-start.137 = (f32[1,512]{1,0:T(1,128)}, f32[1,512]{1,0:T(1,128)S(1)}, u32[]{:S(2)}) copy-start(f32[1,512]{1,0:T(1,128)S(1)} %get-tuple-element.2215) | copy-start | bytes 6148 | tf_op jit(solution)/shard_map/cond
  707.5 28.3 %copy-start.139 = (f32[1,512]{1,0:T(1,128)}, f32[1,512]{1,0:T(1,128)S(1)}, u32[]{:S(2)}) copy-start(f32[1,512]{1,0:T(1,128)S(1)} %get-tuple-element.2216) | copy-start | bytes 6148 | tf_op jit(solution)/shard_map/cond
  707.5 28.3 %copy-start.141 = (f32[1,512]{1,0:T(1,128)}, f32[1,512]{1,0:T(1,128)S(1)}, u32[]{:S(2)}) copy-start(f32[1,512]{1,0:T(1,128)S(1)} %get-tuple-element.2217) | copy-start | bytes 6148 | tf_op jit(solution)/shard_map/cond
  707.5 28.3 %copy-start.143 = (f32[1,512]{1,0:T(1,128)}, f32[1,512]{1,0:T(1,128)S(1)}, u32[]{:S(2)}) copy-start(f32[1,512]{1,0:T(1,128)S(1)} %get-tuple-element.2218) | copy-start | bytes 6148 | tf_op jit(solution)/shard_map/cond
  716.3 9.6 copy-start.89
  765.2 13.8 copy-start.138
  765.3 13.8 copy-start.140
  765.3 13.8 copy-start.142
  765.3 13.8 copy-start.144
  791.9 6.9 slice-start.2
  829.7 111.2 %reduce-scatter.48.cloned.1.call-start = ((), (), s32[]{:S(2)}) async-start(), calls=%async_computation.30 | async-start | bytes 278528
  831.4 167.5 %reduce-scatter.50.cloned.1.call-start = ((), (), s32[]{:S(2)}) async-start(), calls=%async_computation.31 | async-start | bytes 278528
  833.0 223.6 %reduce-scatter.54.cloned.1.call-start = ((), (), s32[]{:S(2)}) async-start(), calls=%async_computation.33 | async-start | bytes 278528
  834.6 279.9 %reduce-scatter.56.cloned.1.call-start = ((), (), s32[]{:S(2)}) async-start(), calls=%async_computation.34 | async-start | bytes 278528
  836.2 336.0 %reduce-scatter.58.cloned.1.call-start = ((), (), s32[]{:S(2)}) async-start(), calls=%async_computation.35 | async-start | bytes 278528
  841.2 388.9 %reduce-scatter.52.cloned.1.call-start = ((), (), s32[]{:S(2)}) async-start(), calls=%async_computation.32 | async-start | bytes 278528
  845.4 445.2 %reduce-scatter.36.cloned.1.call-start = ((), (), s32[]{:S(2)}) async-start(), calls=%async_computation.24 | async-start | bytes 1114112 | tf_op jit(solution)/shard_map/reduce_scatter | solution.py:471
  846.0 505.6 %reduce-scatter.40.cloned.1.call-start = ((), (), s32[]{:S(2)}) async-start(), calls=%async_computation.26 | async-start | bytes 1114112 | tf_op jit(solution)/shard_map/reduce_scatter | solution.py:476
  846.6 569.8 %reduce-scatter.38.cloned.1.call-start = ((), (), s32[]{:S(2)}) async-start(), calls=%async_computation.25 | async-start | bytes 2228224 | tf_op jit(solution)/shard_map/reduce_scatter | solution.py:473
  847.2 639.2 %reduce-scatter.34.cloned.1.call-start = ((), (), s32[]{:S(2)}) async-start(), calls=%async_computation.23 | async-start | bytes 3342336 | tf_op jit(solution)/shard_map/reduce_scatter | solution.py:470
  847.8 714.8 %reduce-scatter.30.cloned.1.call-start = ((), (), s32[]{:S(2)}) async-start(), calls=%async_computation.21 | async-start | bytes 4456448 | tf_op jit(solution)/shard_map/reduce_scatter | solution.py:467
  848.3 790.1 %reduce-scatter.42.cloned.1.call-start = ((), (), s32[]{:S(2)}) async-start(), calls=%async_computation.27 | async-start | bytes 4456448 | tf_op jit(solution)/shard_map/reduce_scatter | solution.py:478
  849.1 865.6 %reduce-scatter.32.cloned.1.call-start = ((), (), s32[]{:S(2)}) async-start(), calls=%async_computation.22 | async-start | bytes 4456448 | tf_op jit(solution)/shard_map/reduce_scatter | solution.py:468
  854.6 936.1 %reduce-scatter.44.cloned.1.call-start = ((), (), s32[]{:S(2)}) async-start(), calls=%async_computation.28 | async-start | bytes 4456448 | tf_op jit(solution)/shard_map/reduce_scatter | solution.py:479
  860.1 11.4 copy-start
  860.1 11.4 copy-start.7
  860.1 11.4 copy-start.8
  860.2 11.4 copy-start.47
  877.7 912.9 %copy-start.80 = (bf16[1,2,1,384,512]{4,3,2,1,0:T(8,128)(2,1)}, bf16[1,2,1,384,512]{4,3,2,1,0:T(8,128)(2,1)S(1)}, u32[]{:S(2)}) copy-start(bf16[1,2,1,384,512]{4,3,2,1,0:T(8,128)(2,1)S(1)} %bitcast_dynamic-update-slice_fusion.1) | copy-start | bytes 2359300
  (140 other events, 320.1 us)
Sparse Core Ops, SparseCore 0:
  10.2 40.8 all-gather.12
  53.3 38.5 all-gather.10
  94.1 41.6 all-gather.6
  137.8 40.4 all-gather.8
  180.3 40.1 all-gather.14
  222.5 40.1 all-gather.16
  829.9 53.1 reduce-scatter.45
  886.6 54.3 reduce-scatter.47
  944.5 54.3 reduce-scatter.49
  1002.2 54.3 reduce-scatter.53
  1060.1 54.3 reduce-scatter.55
  1117.8 54.3 reduce-scatter.57
  1175.7 54.3 reduce-scatter.51
  1234.2 56.4 reduce-scatter.35
  1295.1 56.4 reduce-scatter.39
  1355.8 60.5 reduce-scatter.37
  1421.1 65.2 reduce-scatter.33
  1491.1 71.3 reduce-scatter.29
  1567.0 71.4 reduce-scatter.41
  1643.2 71.4 reduce-scatter.31
  1719.1 71.4 reduce-scatter.43
where the time goes:
time: 1810 us; the launch traced here: 1800 us
  waiting for transfers between devices  1150 us (64%)
  other arithmetic  199 us (11%)
  matrix products  180 us (10%)
  local copies, waits for them, and re-layouts  113 us (6%)
  blocking collectives  97.4 us (5%)
  between operations  23.9 us (1%)
  loops' own time  23.3 us (1%)
    unnamed x28, waiting for transfers between devices  352 us
    ppermute x4, waiting for transfers between devices, shifted(): return lax.ppermute(block, axis, route)  109 us
    reduce_scatter x1, waiting for transfers between devices, body(): lax.psum_scatter(totals[2][None], 'dp', scatter_dimension=2, tiled=True)  76.3 us
    reduce_scatter x1, waiting for transfers between devices, body(): lax.psum_scatter(totals[1][None], 'dp', scatter_dimension=1, tiled=True)  76.2 us
    reduce_scatter x1, waiting for transfers between devices, body(): lax.psum_scatter(totals[13][None], 'dp', scatter_dimension=2, tiled=True)  75.9 us
    reduce_scatter x1, waiting for transfers between devices, body(): lax.psum_scatter(totals[12][None], 'dp', scatter_dimension=1, tiled=True)  75.9 us
    dot_general x16, matrix products, weight_product(): jnp.einsum('ulk,uln->kn', left, grads, preferred_element_type=jnp.float32)  74.1 us
    reduce_scatter x1, waiting for transfers between devices, body(): lax.psum_scatter(totals[4][None], 'dp', scatter_dimension=1, tiled=True)  70 us
  transfers between devices with their start and end apart: 25, of which 23 were waited for; matrix products, arithmetic and copies ran while one was open for 4% of the time, Pallas kernels for 0%

commit v1 on v0

v1 whole, which is shorter than its diff:
```python
import functools
import math

import jax
import jax.numpy as jnp
import numpy as np
from jax import lax
from jax.experimental import pallas as pl
from jax.experimental.pallas import tpu as pltpu
from jax.sharding import PartitionSpec as P

HEADS = 8
KERNEL = 15
EPSILON = 1e-05
LOW = jnp.bfloat16
F32 = jnp.float32

EU, ED, PJ, AO, CI, CO, LU, LD, SM = 0, 2048, 4096, 5632, 6144, 7168, 7680, 9728, 11776
COLS = 11904
STEP = 512
G_EARLY, G_ATTEND, G_CONV, G_MIX, G_LATE, G_FINAL, TAPS = 0, 1, 2, 3, 4, 5, 6


def dot(left, right):
    return lax.dot_general(left, right, (((1,), (0,)), ((), ())), preferred_element_type=F32)


def dot_t(left, right):
    return lax.dot_general(left, right, (((1,), (1,)), ((), ())), preferred_element_type=F32)


def sigmoid(values):
    return 0.5 * jnp.tanh(0.5 * values) + 0.5


def norm_hat(values):
    center = values - jnp.mean(values, axis=-1, keepdims=True)
    rate = lax.rsqrt(jnp.mean(center * center, axis=-1, keepdims=True) + EPSILON)
    return center * rate, rate


def norm_grad(grad_hat, hat, rate):
    first = jnp.mean(grad_hat, axis=-1, keepdims=True)
    second = jnp.mean(grad_hat * hat, axis=-1, keepdims=True)
    return rate * (grad_hat - first - hat * second)


class Layer:
    def __init__(self, refs, emit):
        self.__dict__.update(refs)
        self.emit = emit

    def gain(self, l, row):
        return self.sm[l, row : row + 1, :]

    def weight(self, l, column, size=STEP):
        return self.w[l, :, column : column + size]

    def enter(self, l, site, row):
        values = self.stream[...]
        hat, rate = norm_hat(values)
        self.xh[l, site] = hat.astype(LOW)
        self.rate[l, :, site : site + 1] = rate
        return (hat * self.gain(l, row)).astype(LOW)

    def leave(self, l, site, row, grad):
        hat = self.xh[l, site].astype(F32)
        rate = self.rate[l, :, site : site + 1]
        self.smg[l, row : row + 1, :] = jnp.sum(grad * hat, axis=0, keepdims=True)
        return norm_grad(grad * self.gain(l, row), hat, rate)

    def small_forward(self, l):
        block = self.w[l, :, SM : SM + 128].astype(F32)
        self.sm[l] = block.T[:32]

    def small_backward(self, l):
        self.emit(l, SM, self.smg[l].T)

    def feed_forward(self, l, site, row, place, up, down):
        normed = self.enter(l, site, row)
        self.at[l, place] = normed.T
        side = 0 if site == 0 else 1
        total = None
        for j in range(0, 2048, STEP):
            inner = dot(normed, self.weight(l, up + j))
            self.u[l, side, :, j : j + STEP] = inner.astype(LOW)
            hidden = (inner * sigmoid(inner)).astype(LOW)
            term = dot_t(hidden, self.weight(l, down + j))
            total = term if total is None else total + term
        self.stream[...] += 0.5 * total

    def feed_backward(self, l, site, row, place, up, down):
        branch = (0.5 * self.grad[...]).astype(LOW)
        turned = branch.T
        side = 0 if site == 0 else 1
        total = None
        for j in range(0, 2048, STEP):
            hidden_grad = dot(branch, self.weight(l, down + j))
            inner = self.u[l, side, :, j : j + STEP].astype(F32)
            gate = sigmoid(inner)
            hidden = inner * gate
            inner_grad = (hidden_grad * (gate + hidden * (1.0 - gate))).astype(LOW)
            self.emit(l, down + j, dot(turned, hidden.astype(LOW)))
            self.emit(l, up + j, dot(self.at[l, place], inner_grad))
            term = dot_t(inner_grad, self.weight(l, up + j))
            total = term if total is None else total + term
        self.grad[...] += self.leave(l, site, row, total)

    def rotate(self, values, sign):
        cosine, sine = self.cos[...], self.sin[...]
        if sign < 0:
            sine = -sine
        parts = []
        for g in range(0, 512, 256):
            front, behind = values[:, g : g + 128], values[:, g + 128 : g + 256]
            parts += [front * cosine - behind * sine, front * sine + behind * cosine]
        return parts

    def pair_mask(self, j):
        lane = lax.broadcasted_iota(jnp.int32, (1, 256), 1)
        return (lane % 128) // 32 == j

    def head_mask(self, j):
        lane = lax.broadcasted_iota(jnp.int32, (1, 256), 1)
        return lane // 64 == j

    def attend_forward(self, l):
        normed = self.enter(l, 1, G_ATTEND)
        self.at[l, 1] = normed.T
        for which, scale in ((0, 0.125), (1, 1.0)):
            parts = self.rotate(dot(normed, self.weight(l, PJ + 512 * which)), 1)
            for i, part in enumerate(parts):
                self.qkv[l, which, :, 128 * i : 128 * i + 128] = part.astype(LOW) * LOW(scale)
        self.kt[l] = self.qkv[l, 1].T
        value_rows = dot(normed, self.weight(l, PJ + 1024)).astype(LOW)
        self.qkv[l, 2] = value_rows
        self.vt[...] = value_rows.T
        for h in range(HEADS):
            g, j = h // 4 * 256, h % 4
            keys = self.qkv[l, 1, :, g : g + 256]
            keys = jnp.where(self.pair_mask(j), keys, jnp.zeros_like(keys))
            scores = dot_t(keys, self.qkv[l, 0, :, g : g + 256]) + self.bias[...]
            powers = jnp.exp(scores - jnp.max(scores, axis=0, keepdims=True))
            powers = powers * (1.0 / jnp.sum(powers, axis=0, keepdims=True))
            powers = powers.astype(LOW)
            self.pt[l, h] = powers
            self.ot[l, 64 * h : 64 * h + 64, :] = dot(
                self.vt[64 * h : 64 * h + 64, :], powers
            ).astype(LOW)
        self.stream[...] += dot(self.ot[l].T, self.weight(l, AO))

    def attend_backward(self, l):
        branch = self.grad[...].astype(LOW)
        self.emit(l, AO, dot(self.ot[l], branch))
        self.ctx[...] = dot_t(branch, self.weight(l, AO)).astype(LOW)
        key_total, value_total = [], []
        for g in range(0, 512, 256):
            ctx = self.ctx[:, g : g + 256]
            queries = self.qkv[l, 0, :, g : g + 256]
            values = self.qkv[l, 2, :, g : g + 256]
            key_grad = value_grad = None
            for j in range(4):
                h = g // 64 + j
                head = self.head_mask(j)
                soft_grad = dot_t(jnp.where(head, values, jnp.zeros_like(values)), ctx)
                soft_low = self.pt[l, h]
                soft = soft_low.astype(F32)
                delta = jnp.sum(soft_grad * soft, axis=0, keepdims=True)
                score_grad = (soft * (soft_grad - delta)).astype(LOW)
                term = dot(soft_low, jnp.where(head, ctx, jnp.zeros_like(ctx)))
                value_grad = term if value_grad is None else value_grad + term
                term = dot(
                    score_grad, jnp.where(self.pair_mask(j), queries, jnp.zeros_like(queries))
                )
                key_grad = term if key_grad is None else key_grad + term
                front, behind = g + 32 * j, g + 128 + 32 * j
                rows = jnp.concatenate(
                    [self.kt[l, front : front + 32, :], self.kt[l, behind : behind + 32, :]], axis=0
                )
                turned = dot(rows, score_grad)
                self.qt[front : front + 32, :] = turned[:32]
                self.qt[behind : behind + 32, :] = turned[32:]
            key_total.append(key_grad)
            value_total.append(value_grad)
        query_grad = self.qt[...].T * 0.125
        query_grad = jnp.concatenate(self.rotate(query_grad, -1), axis=1).astype(LOW)
        key_grad = jnp.concatenate(key_total, axis=1)
        key_grad = jnp.concatenate(self.rotate(key_grad, -1), axis=1).astype(LOW)
        value_grad = jnp.concatenate(value_total, axis=1).astype(LOW)
        total = None
        for i, part in enumerate((query_grad, key_grad, value_grad)):
            self.emit(l, PJ + 512 * i, dot(self.at[l, 1], part))
            term = dot_t(part, self.weight(l, PJ + 512 * i))
            total = term if total is None else total + term
        self.grad[...] += self.leave(l, 1, G_ATTEND, total)

    def tap(self, l, k):
        row = self.sm[l, TAPS + k : TAPS + k + 1, :]
        return row if k <= KERNEL // 2 else row * self.whole

    def convolve_forward(self, l):
        normed = self.enter(l, 2, G_CONV)
        self.at[l, 2] = normed.T
        first = dot(normed, self.weight(l, CI))
        second = dot(normed, self.weight(l, CI + 512))
        self.gates[l, :, :512] = first.astype(LOW)
        self.gates[l, :, 512:] = second.astype(LOW)
        n = first.shape[0]
        self.pad[0, 8 : n + 8, :] = first * sigmoid(second) * self.live[...]
        mixed = None
        for k in range(KERNEL):
            term = self.tap(l, k) * self.pad[0, k + 1 : k + 1 + n, :]
            mixed = term if mixed is None else mixed + term
        hat, rate = norm_hat(mixed)
        self.xh[l, 5] = hat.astype(LOW)
        self.rate[l, :, 5:6] = rate
        inner = hat * self.gain(l, G_MIX)
        hidden = (inner * sigmoid(inner)).astype(LOW)
        self.wt[l] = hidden.T
        self.stream[...] += dot(hidden, self.weight(l, CO))

    def convolve_backward(self, l):
        branch = self.grad[...].astype(LOW)
        n = branch.shape[0]
        self.emit(l, CO, dot(self.wt[l], branch))
        hidden_grad = dot_t(branch, self.weight(l, CO))
        hat = self.xh[l, 5].astype(F32)
        inner = hat * self.gain(l, G_MIX)
        gate = sigmoid(inner)
        inner_grad = hidden_grad * (gate + inner * gate * (1.0 - gate))
        self.pad[1, 8 : n + 8, :] = self.leave(l, 5, G_MIX, inner_grad)
        first = self.gates[l, :, :512].astype(F32)
        gate = sigmoid(self.gates[l, :, 512:].astype(F32))
        self.pad[0, 8 : n + 8, :] = first * gate * self.live[...]
        mixed_grad = self.pad[1, 8 : n + 8, :]
        total = None
        for k in range(KERNEL):
            row = jnp.sum(mixed_grad * self.pad[0, k + 1 : k + 1 + n, :], axis=0, keepdims=True)
            if k > KERNEL // 2:
                row = row * self.whole
            self.smg[l, TAPS + k : TAPS + k + 1, :] = row
            term = self.tap(l, k) * self.pad[1, 15 - k : 15 - k + n, :]
            total = term if total is None else total + term
        total = total * self.live[...]
        first_grad = (total * gate).astype(LOW)
        second_grad = (total * first * gate * (1.0 - gate)).astype(LOW)
        self.emit(l, CI, dot(self.at[l, 2], first_grad))
        self.emit(l, CI + 512, dot(self.at[l, 2], second_grad))
        total = dot_t(first_grad, self.weight(l, CI))
        total = total + dot_t(second_grad, self.weight(l, CI + 512))
        self.grad[...] += self.leave(l, 2, G_CONV, total)

    def prepare(self, length, flag, span):
        n = self.stream.shape[0]
        key = lax.broadcasted_iota(jnp.int32, (n, n), 0)
        query = lax.broadcasted_iota(jnp.int32, (n, n), 1)
        width = span.astype(F32)
        key_block = jnp.floor((key.astype(F32) + 0.5) / width)
        query_block = jnp.floor((query.astype(F32) + 0.5) / width)
        shown = (key < length) & ((flag == 0) | (key_block <= query_block))
        self.bias[...] = jnp.where(shown, 0.0, -1e30)
        place = lax.broadcasted_iota(jnp.int32, (n, 1), 0)
        self.live[...] = (place < length).astype(F32)
        self.whole = jnp.where(flag == 0, 1.0, 0.0)
        self.pad[...] = jnp.zeros_like(self.pad)
        self.smg[...] = jnp.zeros_like(self.smg)

    def finish_forward(self, l):
        hat, rate = norm_hat(self.stream[...])
        self.xh[l, 4] = hat.astype(LOW)
        self.rate[l, :, 4:5] = rate
        return (hat * self.gain(l, G_FINAL)).astype(LOW)


def act_shapes(n):
    return dict(
        w=pltpu.VMEM((2, 512, COLS), LOW),
        stream=pltpu.VMEM((n, 512), F32),
        grad=pltpu.VMEM((n, 512), F32),
        xh=pltpu.VMEM((2, 6, n, 512), LOW),
        rate=pltpu.VMEM((2, n, 128), F32),
        at=pltpu.VMEM((2, 4, 512, n), LOW),
        u=pltpu.VMEM((2, 2, n, 2048), LOW),
        qkv=pltpu.VMEM((2, 3, n, 512), LOW),
        kt=pltpu.VMEM((2, 512, n), LOW),
        vt=pltpu.VMEM((512, n), LOW),
        qt=pltpu.VMEM((512, n), F32),
        ctx=pltpu.VMEM((n, 512), LOW),
        pt=pltpu.VMEM((2, HEADS, n, n), LOW),
        ot=pltpu.VMEM((2, 512, n), LOW),
        gates=pltpu.VMEM((2, n, 1024), LOW),
        wt=pltpu.VMEM((2, 512, n), LOW),
        pad=pltpu.VMEM((2, n + 16, 512), F32),
        sm=pltpu.VMEM((2, 32, 512), F32),
        smg=pltpu.VMEM((2, 128, 512), F32),
        bias=pltpu.VMEM((n, n), F32),
        live=pltpu.VMEM((n, 1), F32),
    )


def compute_kernel(names, scalars, w_hbm, frames, cotangent, cos, sin, y_out, dx_out, g_out, *scratch):
    refs = dict(zip(names, scratch))
    slots, slot_sem, load_sem = scratch[len(names) :]
    refs.update(cos=cos, sin=sin)
    pending = [None, None]
    count = [0]

    def emit(l, column, value):
        slot = count[0] % 2
        count[0] += 1
        if pending[slot] is not None:
            pending[slot].wait()
        width = value.shape[1]
        slots[slot, :, :width] = value.astype(LOW)
        copy = pltpu.make_async_copy(
            slots.at[slot, :, pl.ds(0, width)],
            g_out.at[l, :, pl.ds(column, width)],
            slot_sem.at[slot],
        )
        copy.start()
        pending[slot] = copy

    run = Layer(refs, emit)
    loads = [pltpu.make_async_copy(w_hbm.at[l], run.w.at[l], load_sem.at[l]) for l in range(2)]
    for load in loads:
        load.start()
    run.prepare(scalars[0], scalars[1], scalars[2])
    run.stream[...] = frames[...].astype(F32)
    for l in range(2):
        loads[l].wait()
        run.small_forward(l)
        run.feed_forward(l, 0, G_EARLY, 0, EU, ED)
        run.attend_forward(l)
        run.convolve_forward(l)
        run.feed_forward(l, 3, G_LATE, 3, LU, LD)
        result = run.finish_forward(l)
        y_out[l] = result
        if l == 0:
            run.stream[...] = result.astype(F32)
    for l in (1, 0):
        start = cotangent[...].astype(F32) if l == 1 else run.grad[...].astype(LOW).astype(F32)
        run.grad[...] = run.leave(l, 4, G_FINAL, start)
        run.feed_backward(l, 3, G_LATE, 3, LU, LD)
        run.convolve_backward(l)
        run.attend_backward(l)
        run.feed_backward(l, 0, G_EARLY, 0, EU, ED)
        run.small_backward(l)
        dx_out[l] = run.grad[...].astype(LOW)
    for copy in pending:
        copy.wait()


def tables(n):
    rates = np.exp(np.arange(32, dtype=np.float64) * (-2.0 * math.log(10000.0) / 64))
    phases = np.arange(n, dtype=np.float64)[:, None] * np.tile(rates, 4)[None, :]
    return np.cos(phases).astype(np.float32), np.sin(phases).astype(np.float32)


def compute(scalars, weights, frames, cotangent):
    n = frames.shape[0]
    shapes = act_shapes(n)
    cosine, sine = tables(n)
    vmem = pl.BlockSpec(memory_space=pltpu.VMEM)
    hbm = pl.BlockSpec(memory_space=pl.ANY)
    return pl.pallas_call(
        functools.partial(compute_kernel, tuple(shapes)),
        out_shape=(
            jax.ShapeDtypeStruct((2, n, 512), LOW),
            jax.ShapeDtypeStruct((2, n, 512), LOW),
            jax.ShapeDtypeStruct((2, 512, COLS), LOW),
        ),
        in_specs=[pl.BlockSpec(memory_space=pltpu.SMEM), hbm, vmem, vmem, vmem, vmem],
        out_specs=(vmem, vmem, hbm),
        scratch_shapes=list(shapes.values())
        + [
            pltpu.VMEM((2, 512, STEP), LOW),
            pltpu.SemaphoreType.DMA((2,)),
            pltpu.SemaphoreType.DMA((2,)),
        ],
        compiler_params=pltpu.CompilerParams(vmem_limit_bytes=62 * 2**20),
        cost_estimate=pl.CostEstimate(
            flops=30 * 10**9, bytes_accessed=60 * 2**20, transcendentals=10**7
        ),
    )(scalars, weights, frames, cotangent, jnp.asarray(cosine), jnp.asarray(sine))


def swap_halves(columns, back=False):
    rows = columns.shape[0]
    shape = (rows, 4, 2, 4, 32) if back else (rows, 4, 4, 2, 32)
    return columns.reshape(shape).swapaxes(2, 3).reshape(rows, 1024)


def pack(shards):
    eg, eu, ed, ag, pj, ao, cg, ci, cd, cn, co, lg, lu, ld, fg = (piece[0] for piece in shards)
    rows = eu.shape[0]
    small = jnp.concatenate(
        [gain[:, None] for gain in (eg, ag, cg, cn, lg, fg)]
        + [cd.T, jnp.zeros((rows, 128 - 6 - KERNEL), LOW)],
        axis=1,
    )
    proj = jnp.concatenate([swap_halves(pj[:, :1024]), pj[:, 1024:]], axis=1)
    return jnp.concatenate([eu, ed.T, proj, ao, ci, co, lu, ld.T, small], axis=1)


def unpack(block):
    proj = block[:, PJ : PJ + 1536]
    proj = jnp.concatenate([swap_halves(proj[:, :1024], True), proj[:, 1024:]], axis=1)
    gains = [block[:, SM + i] for i in range(6)]
    eg, ag, cg, cn, lg, fg = gains
    outs = (
        eg,
        block[:, EU:ED],
        block[:, ED:PJ].T,
        ag,
        proj,
        block[:, AO:CI],
        cg,
        block[:, CI:CO],
        block[:, SM + TAPS : SM + TAPS + KERNEL].T,
        cn,
        block[:, CO:LU],
        lg,
        block[:, LU:LD],
        block[:, LD:SM].T,
        fg,
    )
    return tuple(piece[None] for piece in outs)


def place_pair(own_pair, section):
    own = jnp.where(section == 0, own_pair[0], own_pair[1])
    other = jnp.where(section == 0, own_pair[1], own_pair[0])
    got = lax.ppermute(other, "pipe", [(0, 1), (1, 0)])
    return jnp.where(section == 0, jnp.stack([own, got]), jnp.stack([got, own]))[None, :, None]


def body(frames, cotangent, lengths, stream_flags, span_sizes, *shards):
    section = lax.axis_index("pipe")
    devices = lax.axis_size("dp")

    def mine(block):
        return lax.dynamic_index_in_dim(block, section, 0, keepdims=False)[0]

    scalars = jnp.stack([mine(lengths), mine(stream_flags), mine(span_sizes)])
    packed = pack(shards)
    rows = packed.shape[0]
    full = lax.all_gather(packed, ("pipe", "dp"), axis=0, tiled=True).reshape(2, 512, COLS)
    ys, dxs, grads = compute(scalars, full, mine(frames), mine(cotangent))
    summed = lax.psum_scatter(
        grads.reshape(1024, COLS), ("pipe", "dp"), scatter_dimension=0, tiled=True
    ).astype(F32)
    return (place_pair(ys, section), place_pair(dxs, section)) + unpack(summed)


def solution(mesh):
    gain, matrix, column = P("pipe", "dp"), P("pipe", "dp", None), P("pipe", None, "dp")
    weights = (gain, matrix, column, gain, matrix, matrix, gain, matrix, column, gain, matrix)
    weights = weights + (gain, matrix, column, gain)
    frames, stacked = P(None, "dp", None, None), P("pipe", None, "dp", None, None)
    return jax.shard_map(
        body,
        mesh=mesh,
        in_specs=(frames, frames) + (P(None, "dp"),) * 3 + weights,
        out_specs=(stacked, stacked) + weights,
        check_vma=False,
    )
```

time: 1810 us -> 541 us (0.30)
  waiting for transfers between devices: 1150 us -> 378 us
  other arithmetic: 199 us -> 5.75 us
  matrix products: 180 us -> 0 us
  blocking collectives: 97.4 us -> 0 us
  Pallas kernels: 0 us -> 93.9 us
  local copies, waits for them, and re-layouts: 113 us -> 36.8 us
  loops' own time: 23.3 us -> 0 us
    reduce_scatter x8 -> x0, waiting for transfers between devices: 559 us -> none  [the longest x1 76.3 us: body(): lax.psum_scatter(totals[2][None], 'dp', scatter_dimension=2, tiled=True)]
    dot_general x72 -> x0, matrix products: 165 us -> none  [the longest x16 74.1 us: weight_product(): jnp.einsum('ulk,uln->kn', left, grads, preferred_element_type=jnp.float32)]
    unnamed x28 -> x3, waiting for transfers between devices: 352 us -> 215 us
    pallas_call x0 -> x1, Pallas kernels: none -> 93.9 us  [compute(): pl.pallas_call(functools.partial(compute_kernel, tuple(shapes)), out_shap...]
    ppermute x4 -> x2, waiting for transfers between devices: 109 us -> 16.6 us  [place_pair(): got = lax.ppermute(other, 'pipe', [(0, 1), (1, 0)])]
    mul x34 -> x0, other arithmetic: 66.7 us -> none  [the longest x24 61.6 us: convolve_tail(): depth_taps[offset][None, None, :] * tap_live[:, offset][:, None, None]]
    all_gather x3 -> x0, blocking collectives: 66.2 us -> none  [the longest x1 24 us: fetch_once(): lax.all_gather(shards[8], 'dp', axis=2, tiled=True)]
    convert_element_type x49 -> x1, other arithmetic: 32.2 us -> 0.42 us  [body(): summed = lax.psum_scatter(grads.reshape(1024, COLS), ('pipe', 'dp'), scat...]
  transfers between devices with their start and end apart: 25 -> 4, of which waited for: 23 -> 4; matrix products, arithmetic and copies ran while one was open for 4% -> 2% of each run, Pallas kernels for 0% -> 0%
where the time goes in v1:
time: 541 us; the launch traced here: 532 us
  waiting for transfers between devices  378 us (70%)
  Pallas kernels  93.9 us (17%)
  local copies, waits for them, and re-layouts  36.8 us (7%)
  between operations  14.4 us (3%)
  other arithmetic  5.75 us (1%)
    unnamed x3, waiting for transfers between devices  215 us
    all_gather x1, waiting for transfers between devices, body(): lax.all_gather(packed, ('pipe', 'dp'), axis=0, tiled=True)  147 us
    pallas_call x1, Pallas kernels, compute(): pl.pallas_call(functools.partial(compute_kernel, tuple(shapes)), out_shap...  93.9 us
    ppermute x2, waiting for transfers between devices, place_pair(): got = lax.ppermute(other, 'pipe', [(0, 1), (1, 0)])  16.6 us
    unnamed x18, local copies, waits for them, and re-layouts  15.9 us
  transfers between devices with their start and end apart: 4, of which 4 were waited for; matrix products, arithmetic and copies ran while one was open for 2% of the time, Pallas kernels for 0%

profile of v1, /device:TPU:0, one launch (start us, length us, event | category | flops | bytes accessed | tf_op | source)
XLA Modules:
  0.0 531.6 jit_solution(1518462339111737306)
XLA Ops:
  7.2 0.0 copy-start
  7.2 0.0 all-gather.2.cloned.1.call-start
  7.3 0.8 slice.96
  8.0 0.8 slice.95
  8.9 0.7 copy.69
  9.6 0.8 copy.70
  10.4 0.8 copy.71
  11.1 0.8 copy.68
  11.9 0.8 copy.72
  12.6 0.8 copy.73
  13.4 0.8 copy.74
  14.1 0.2 reshape.172
  14.3 0.1 copy.67
  14.4 0.3 reshape.173
  14.7 2.0 concatenate.34
  16.7 0.0 all-gather.2.cloned.1.call-update
  16.7 0.0 reduce-scatter.4.cloned.1.call-start
  16.8 0.0 copy-done
  16.8 0.6 constant_dynamic-slice_fusion.2
  17.4 1.3 constant_dynamic-slice_fusion
  18.7 2.5 pad_add_fusion.scalars
  21.2 2.0 dynamic-slice_bitcast_fusion
  23.2 147.2 %all-gather.2.cloned.1.call-done = bf16[1024,11904]{1,0:T(8,128)(2,1)} async-done(((bf16[32,11904]{1,0:T(8,128)(2,1)}), bf16[1024,11904]{1,0:T(8,128)(2,1)}) %all-gather.2.cloned.1.call-update) | async-done | bytes 24379408 | tf_op jit(solution)/shard_map/all_gather | solution.py:447
  170.5 93.9 %shard_map.341 = (bf16[2,384,512]{2,1,0:T(8,128)(2,1)}, bf16[2,384,512]{2,1,0:T(8,128)(2,1)}, bf16[2,512,11904]{2,1,0:T(8,128)(2,1)}) custom-call(s32[3]{0:T(128)} %pad_add_fusion.scalars, bf16[2,512,11904]{2,1,0:T(8,128)(2,1)} %bitcast.102, bf16[384,512]{1,0:T(8,128)(2,1)} %get-tuple-element.74.frames, bf16[384,512]{1,0:T(8,128)(2,1)} %get-tuple-element.73.cotangent, ...), custom_call_target="tpu_custom_call" | custom-call | flops 30000001024 | bytes 62914560 | tf_op jit(solution)/shard_map/pallas_call | solution.py:365
  264.3 0.0 copy-start.3
  264.4 0.0 copy-start.2
  264.4 0.0 reduce-scatter.4.cloned.1.call-update
  264.4 1.1 copy-done.3
  265.5 0.1 select_bitcast_fusion.3
  265.5 1.5 collective-permute-start
  267.0 0.0 copy-done.2
  267.0 0.1 select_bitcast_fusion.1
  267.1 0.7 collective-permute-start.1
  267.8 9.8 %collective-permute-done = bf16[384,512]{1,0:T(8,128)(2,1)S(1)} collective-permute-done((bf16[384,512]{1,0:T(8,128)(2,1)S(1)}, bf16[384,512]{1,0:T(8,128)(2,1)S(1)}, u32[]{:S(2)}, u32[]{:S(2)}) %collective-permute-start) | collective-permute-done | bytes 393248 | tf_op jit(solution)/shard_map/ppermute | solution.py:433
  277.6 1.0 maximum_select_fusion
  278.6 6.8 %collective-permute-done.1 = bf16[384,512]{1,0:T(8,128)(2,1)S(1)} collective-permute-done((bf16[384,512]{1,0:T(8,128)(2,1)S(1)}, bf16[384,512]{1,0:T(8,128)(2,1)S(1)}, u32[]{:S(2)}, u32[]{:S(2)}) %collective-permute-start.1) | collective-permute-done | bytes 393248 | tf_op jit(solution)/shard_map/ppermute | solution.py:433
  285.3 1.0 maximum_select_fusion.1
  286.3 214.7 %reduce-scatter.4.cloned.1.call-done = bf16[32,11904]{1,0:T(8,128)(2,1)} async-done(((bf16[1024,11904]{1,0:T(8,128)(2,1)}), bf16[32,11904]{1,0:T(8,128)(2,1)}) %reduce-scatter.4.cloned.1.call-update) | async-done | bytes 761872
  501.0 2.9 copy.87
  503.9 0.9 slice.101
  504.7 0.4 convert_element_type.3
  505.2 0.5 slice_bitcast_fusion.8
  505.7 0.9 slice_bitcast_fusion.4
  506.6 0.8 slice_bitcast_fusion.5
  507.4 0.0 copy-start.1
  507.4 1.3 slice_bitcast_fusion
  508.6 0.1 copy.77
  508.7 2.3 copy.76
  511.0 1.7 reshape.177
  512.7 0.6 copy.82
  513.3 1.9 copy.81
  515.2 2.2 copy.85
  517.4 1.7 copy.83
  519.1 1.7 copy.80
  520.8 1.0 copy.84
  521.8 1.0 copy.79
  522.8 1.0 copy.78
  523.8 0.7 maximum_bitcast_fusion
  524.5 0.0 copy-done.1
  (3 shorter events, 0.0 us)
Async XLA Ops:
  7.2 9.6 %copy-start = (s32[2,1]{0,1:T(1,128)S(1)}, s32[2,1]{0,1:T(1,128)}, u32[]{:S(2)}) copy-start(s32[2,1]{0,1:T(1,128)} %param.24) | copy-start | bytes 28
  7.2 163.3 %all-gather.2.cloned.1.call-start = ((), (), s32[]{:S(2)}) async-start(), calls=%async_computation.1 | async-start | bytes 25141248 | tf_op jit(solution)/shard_map/all_gather | solution.py:447
  16.7 484.2 %reduce-scatter.4.cloned.1.call-start = ((), (), s32[]{:S(2)}) async-start(), calls=%async_computation.2 | async-start | bytes 25141248
  264.3 1.1 copy-start.3
  264.4 2.7 copy-start.2
  265.5 12.0 %collective-permute-start = (bf16[384,512]{1,0:T(8,128)(2,1)S(1)}, bf16[384,512]{1,0:T(8,128)(2,1)S(1)}, u32[]{:S(2)}, u32[]{:S(2)}) collective-permute-start(bf16[384,512]{1,0:T(8,128)(2,1)S(1)} %get-tuple-element.72), channel_id=1, source_target_pairs={{0,16},{16,0},{1,17},{17,1},{2,18},{18,2},{3,19},{19,3},{4,20},{20... | collective-permute-start | bytes 1179656 | tf_op jit(solution)/shard_map/ppermute | solution.py:433
  267.1 18.2 %collective-permute-start.1 = (bf16[384,512]{1,0:T(8,128)(2,1)S(1)}, bf16[384,512]{1,0:T(8,128)(2,1)S(1)}, u32[]{:S(2)}, u32[]{:S(2)}) collective-permute-start(bf16[384,512]{1,0:T(8,128)(2,1)S(1)} %get-tuple-element.70), channel_id=1, source_target_pairs={{0,16},{16,0},{1,17},{17,1},{2,18},{18,2},{3,19},{19,3},{4,20},{20... | collective-permute-start | bytes 1179656 | tf_op jit(solution)/shard_map/ppermute | solution.py:433
  507.4 17.1 %copy-start.1 = (s32[2,1]{0,1:T(1,128)S(1)}, s32[2,1]{0,1:T(1,128)}, u32[]{:S(2)}) copy-start(s32[2,1]{0,1:T(1,128)} %param.24) | copy-start | bytes 28
Sparse Core Ops, SparseCore 0:
  16.9 153.5 all-gather.1
  264.5 236.4 reduce-scatter.3
